TPU v7x, 32 devices: a whole 2x2x4 slice. The times are simulated.
32 devices in a mesh: batch: 2 (over y), rows: 8 (over z, x), cols: 2 (over core).
Axes of the slice: x: 2, y: 2, z: 4, core: 2. Of those that a mesh axis runs over, the one named last changes fastest.
Arguments:
- features: bfloat16 [8192, 1024], P(('batch', 'rows'), 'cols'), parts along dimension 0, may hold values from -6 to 6
- edge_vals: bfloat16 [64, 8, 128, 128], P(('batch', 'rows')), parts along dimension 0, may hold values from 0.019897461 to 1
- block_cols: int32 [64, 8], P(('batch', 'rows')), parts along dimension 0, may hold values from 0 to 31, as said below
- block_count: int32 [64], P(('batch', 'rows')), parts along dimension 0, may hold values from 1 to 8
- w_self: bfloat16 [1024, 1024], P('rows', 'cols'), may hold values from -0.1875 to 0.1875
- w_neigh: bfloat16 [1024, 1024], P('rows', 'cols'), may hold values from -3 to 3
- cotangent: bfloat16 [8192, 1024], P(('batch', 'rows'), 'cols'), parts along dimension 0, may hold values from -6 to 6
Outputs:
- output: bfloat16 [8192, 1024], P(('batch', 'rows'), 'cols'), parts along dimension 0
- grad_self: float32 [2048, 1024], P(('batch', 'rows'), 'cols'), parts along dimension 0
- grad_neigh: float32 [2048, 1024], P(('batch', 'rows'), 'cols'), parts along dimension 0
There are 2 independent parts, one for each index of `batch`. A program takes and returns all parts, laid end to end along the dimension named above; an argument that names none is the same for every part. Nothing has to cross between parts.
Inputs may be any that keep to these rules, and one draw needn't show every extreme that they name: `block_cols`: each entry names a row block whose device along rows lies within 2 devices of the row block's own device; slot 0 names the row block itself.
All inputs are finite; a program needn't handle non-finite values.
Results may differ from a plain program's by a relative error of at most 0.0056.
Values may be sent and summed in bfloat16 or wider, within the bound.
A program may use at most 64 MiB of HBM per device.

v0:
```python
import math

import jax
import jax.numpy as jnp
from jax import lax
from jax.sharding import PartitionSpec as P

B = 128
REACH = 2


def passed_along(array, axis, by):
    peers = lax.axis_size(axis)
    pairs = [(i, i + by) for i in range(peers) if 0 <= i + by < peers]
    return lax.ppermute(array, axis, pairs)


def local(features, edge_vals, block_cols, block_count, w_self, w_neigh, cotangent):
    node_rows = features.shape[0]
    width = features.shape[1]
    blocks_here = node_rows // B
    slot_count = edge_vals.shape[1]
    pieces_list = []
    for offset in range(-REACH, REACH + 1):
        if offset == 0:
            pieces_list.append(features)
        else:
            pieces_list.append(passed_along(features, "rows", -offset))
    extended = jnp.concatenate(pieces_list, axis=0)
    ext_blocks = extended.reshape(-1, B, width)
    base = (lax.axis_index("rows") - REACH) * blocks_here
    local_cols = block_cols - base
    used = jnp.arange(slot_count)[None, :] < block_count[:, None]
    masked = jnp.where(used[:, :, None, None], edge_vals, jnp.zeros_like(edge_vals))
    degree = jnp.sum(masked.astype(jnp.float32), axis=(1, 3))
    picked = ext_blocks[local_cols]
    summed = jnp.einsum("bkij,bkjf->bif", masked, picked, preferred_element_type=jnp.float32)
    aggregated = (summed / degree[:, :, None]).reshape(node_rows, width).astype(jnp.bfloat16)
    full_feat = lax.all_gather(features, "cols", axis=1, tiled=True)
    full_agg = lax.all_gather(aggregated, "cols", axis=1, tiled=True)

    def add_rows(left, piece):
        return jnp.dot(left, piece, preferred_element_type=jnp.float32)

    self_part = add_rows(full_feat, lax.all_gather(w_self, "rows", axis=0, tiled=True))
    neigh_part = add_rows(full_agg, lax.all_gather(w_neigh, "rows", axis=0, tiled=True))
    pre = self_part + neigh_part
    sigma = jax.nn.sigmoid(pre)
    output = (pre * sigma).astype(jnp.bfloat16)
    grad_pre = (cotangent.astype(jnp.float32) * sigma * (1.0 + pre * (1.0 - sigma))).astype(
        jnp.bfloat16
    )
    inverse = 1.0 / math.sqrt(node_rows * lax.axis_size("rows"))
    grads = lax.psum_scatter(
        jnp.concatenate(
            [
                jnp.einsum("nk,nh->kh", full_feat, grad_pre, preferred_element_type=jnp.float32),
                jnp.einsum("nk,nh->kh", full_agg, grad_pre, preferred_element_type=jnp.float32),
            ],
            axis=1,
        ),
        "rows",
        scatter_dimension=0,
        tiled=True,
    )
    out_cols = grad_pre.shape[1]
    grad_self = grads[:, :out_cols] * inverse
    grad_neigh = grads[:, out_cols:] * inverse
    return (output, grad_self, grad_neigh)


def solution(mesh):
    placed = (
        P(("batch", "rows"), "cols"),
        P(("batch", "rows"), None, None, None),
        P(("batch", "rows"), None),
        P(("batch", "rows")),
        P("rows", "cols"),
        P("rows", "cols"),
        P(("batch", "rows"), "cols"),
    )
    return jax.shard_map(
        local,
        mesh=mesh,
        in_specs=placed,
        out_specs=(
            P(("batch", "rows"), "cols"),
            P(("batch", "rows"), "cols"),
            P(("batch", "rows"), "cols"),
        ),
        check_vma=False,
    )
```

profile of v0, /device:TPU:0, one launch (start us, length us, event | category | flops | bytes accessed | tf_op | source)
XLA Modules:
  0.0 226.2 jit_solution(4661419460646032933)
XLA Ops:
  7.2 0.0 copy-start
  7.2 0.0 all-gather.5.cloned.1.call-start
  7.2 0.7 all-gather.5.cloned.1.call-update
  7.9 0.0 all-gather.7.cloned.1.call-start
  8.0 5.7 %collective-permute-start = (bf16[512,512]{1,0:T(8,128)(2,1)}, bf16[512,512]{1,0:T(8,128)(2,1)}, u32[]{:S(2)}, u32[]{:S(2)}) collective-permute-start(bf16[512,512]{1,0:T(8,128)(2,1)} %param.7), channel_id=1, source_target_pairs={{0,4},{2,6},{4,8},{6,10},{8,12},{10,14},{1,5},{3,7},{5,9},{7,11},{... | collective-permute-start | bytes 1572872 | tf_op jit(solution)/shard_map/ppermute | solution.py:15
  13.7 4.2 %collective-permute-start.1 = (bf16[512,512]{1,0:T(8,128)(2,1)}, bf16[512,512]{1,0:T(8,128)(2,1)}, u32[]{:S(2)}, u32[]{:S(2)}) collective-permute-start(bf16[512,512]{1,0:T(8,128)(2,1)} %param.7), channel_id=1, source_target_pairs={{0,2},{2,4},{4,6},{6,8},{8,10},{10,12},{12,14},{1,3},{3,5},{5,7},{... | collective-permute-start | bytes 1572872 | tf_op jit(solution)/shard_map/ppermute | solution.py:15
  17.9 1.3 collective-permute-start.2
  19.2 1.3 collective-permute-start.3
  20.5 0.0 all-gather.7.cloned.1.call-update
  20.5 0.0 all-gather.9.cloned.1.call-start
  20.5 0.7 compare_select_fusion
  21.2 0.7 iota_compare_fusion
  22.0 1.6 convert_reduce_fusion
  23.5 0.1 reshape.36
  23.6 0.7 collective-permute-done
  24.4 1.1 constant_dynamic-update-slice_fusion.4
  25.4 15.5 %collective-permute-done.1 = bf16[512,512]{1,0:T(8,128)(2,1)} collective-permute-done((bf16[512,512]{1,0:T(8,128)(2,1)}, bf16[512,512]{1,0:T(8,128)(2,1)}, u32[]{:S(2)}, u32[]{:S(2)}) %collective-permute-start.1) | collective-permute-done | bytes 524320 | tf_op jit(solution)/shard_map/ppermute | solution.py:15
  40.9 1.1 constant_dynamic-update-slice_fusion.3
  42.0 0.0 copy-done
  42.1 0.0 collective-permute-done.2
  42.1 1.1 constant_dynamic-update-slice_fusion.1
  43.1 4.5 %collective-permute-done.3 = bf16[512,512]{1,0:T(8,128)(2,1)} collective-permute-done((bf16[512,512]{1,0:T(8,128)(2,1)}, bf16[512,512]{1,0:T(8,128)(2,1)}, u32[]{:S(2)}, u32[]{:S(2)}) %collective-permute-start.3) | collective-permute-done | bytes 524320 | tf_op jit(solution)/shard_map/ppermute | solution.py:15
  47.6 1.1 constant_dynamic-update-slice_fusion
  48.7 2.8 %gather_fusion = bf16[32,128,512]{2,1,0:T(8,128)(2,1)} fusion(bf16[20,128,512]{2,1,0:T(8,128)(2,1)S(1)} %bitcast.19, s32[1024]{0:T(1024)S(1)} %pad_clamp_fusion), kind=kCustom, calls=%fused_computation | custom fusion | bytes 8388736 | tf_op jit(solution)/shard_map/gather | solution.py:36
  51.5 4.2 %fusion.1 = bf16[4,128,512]{2,1,0:T(8,128)(2,1)} fusion(bf16[4,8,128,512]{3,2,1,0:T(8,128)(2,1)} %bitcast.20, bf16[4,8,128,128]{3,2,1,0:T(8,128)(2,1)} %param.8, pred[4,8]{1,0:T(4,128)(4,1)S(1)} %iota_compare_fusion, f32[4,128]{1,0:T(4,128)S(1)} %convert_reduce_fusion), kind=kOutput, calls=%fused_computation.7 | convolution fusion | flops 537919488 | bytes 5769248 | tf_op jit(solution)/shard_map/bkij,bkjf->bif/dot_general | solution.py:37
  55.7 0.0 all-gather.9.cloned.1.call-update
  55.7 0.0 all-gather.11.cloned.1.call-start
  55.7 0.5 all-gather.11.cloned.1.call-update
  56.3 0.0 reduce-scatter.2.cloned.1.call-start
  56.3 0.0 all-gather.5.cloned.1.call-done
  56.3 12.3 %all-gather.7.cloned.1.call-done = bf16[1024,512]{1,0:T(8,128)(2,1)} async-done(((bf16[128,512]{1,0:T(8,128)(2,1)}), bf16[1024,512]{1,0:T(8,128)(2,1)}) %all-gather.7.cloned.1.call-update) | async-done | bytes 1048592 | tf_op jit(solution)/shard_map/all_gather | solution.py:45
  68.6 2.2 fusion.5
  70.9 0.0 copy-start.3
  70.9 7.7 %all-gather.9.cloned.1.call-done = bf16[512,1024]{1,0:T(8,128)(2,1)} async-done(((bf16[512,512]{1,0:T(8,128)(2,1)}), bf16[512,1024]{1,0:T(8,128)(2,1)}) %all-gather.9.cloned.1.call-update) | async-done | bytes 1048592 | tf_op jit(solution)/shard_map/all_gather | solution.py:40
  78.6 0.0 copy-start.2
  78.6 43.3 %all-gather.11.cloned.1.call-done = bf16[1024,512]{1,0:T(8,128)(2,1)} async-done(((bf16[128,512]{1,0:T(8,128)(2,1)}), bf16[1024,512]{1,0:T(8,128)(2,1)}) %all-gather.11.cloned.1.call-update) | async-done | bytes 1048592 | tf_op jit(solution)/shard_map/all_gather | solution.py:46
  121.9 3.2 %multiply_convert_fusion.1 = (bf16[512,512]{1,0:T(8,128)(2,1)}, f32[512,512]{1,0:T(8,128)S(1)}) fusion(f32[512,512]{1,0:T(8,128)S(1)} %fusion.5, bf16[512,1024]{1,0:T(8,128)(2,1)} %all-gather.9.cloned.1.call-done, bf16[1024,512]{1,0:T(8,128)(2,1)} %all-gather.11.cloned.1.call-done), kind=kOutput, calls=%fused_computation.9 | convolution fusion | flops 538443776 | bytes 4718592 | tf_op jit(solution)/shard_map/dot_general | solution.py:43
  125.1 0.0 copy-done.3
  125.1 0.0 copy-done.2
  125.1 0.9 fusion.4
  126.0 0.4 copy-done.1
  126.3 0.9 convolution_bitcast_fusion
  127.2 2.5 %pad_maximum_fusion = f32[1024,1024]{0,1:T(8,128)} fusion(f32[1024,512]{0,1:T(8,128)S(1)} %fusion.4, f32[1024,512]{0,1:T(8,128)S(1)} %convolution_bitcast_fusion), kind=kLoop, calls=%fused_computation.1 | loop fusion | flops 1048576 | bytes 8388608 | tf_op jit(solution)/shard_map/concatenate | solution.py:55
  129.7 0.0 reduce-scatter.2.cloned.1.call-update
  129.7 87.2 %reduce-scatter.2.cloned.1.call-done = f32[128,1024]{0,1:T(8,128)} async-done(((f32[1024,1024]{0,1:T(8,128)}), f32[128,1024]{0,1:T(8,128)}) %reduce-scatter.2.cloned.1.call-update) | async-done | bytes 524304 | tf_op jit(solution)/shard_map/reduce_scatter | solution.py:54
  217.0 1.1 slice_multiply_fusion
  218.0 0.8 copy.10
  218.9 0.8 copy.11
  (3 shorter events, 0.0 us)
Async XLA Ops:
  7.2 34.8 %copy-start = (bf16[512,512]{1,0:T(8,128)(2,1)S(1)}, bf16[512,512]{1,0:T(8,128)(2,1)}, u32[]{:S(2)}) copy-start(bf16[512,512]{1,0:T(8,128)(2,1)} %param.7) | copy-start | bytes 1572868
  7.2 49.1 %all-gather.5.cloned.1.call-start = ((), (), s32[]{:S(2)}) async-start(), calls=%async_computation.1 | async-start | bytes 1572864 | tf_op jit(solution)/shard_map/all_gather | solution.py:39
  7.9 60.7 %all-gather.7.cloned.1.call-start = ((), (), s32[]{:S(2)}) async-start(), calls=%async_computation.2 | async-start | bytes 1179648 | tf_op jit(solution)/shard_map/all_gather | solution.py:45
  8.0 16.4 %collective-permute-start = (bf16[512,512]{1,0:T(8,128)(2,1)}, bf16[512,512]{1,0:T(8,128)(2,1)}, u32[]{:S(2)}, u32[]{:S(2)}) collective-permute-start(bf16[512,512]{1,0:T(8,128)(2,1)} %param.7), channel_id=1, source_target_pairs={{0,4},{2,6},{4,8},{6,10},{8,12},{10,14},{1,5},{3,7},{5,9},{7,11},{... | collective-permute-start | bytes 1572872 | tf_op jit(solution)/shard_map/ppermute | solution.py:15
  13.7 27.2 %collective-permute-start.1 = (bf16[512,512]{1,0:T(8,128)(2,1)}, bf16[512,512]{1,0:T(8,128)(2,1)}, u32[]{:S(2)}, u32[]{:S(2)}) collective-permute-start(bf16[512,512]{1,0:T(8,128)(2,1)} %param.7), channel_id=1, source_target_pairs={{0,2},{2,4},{4,6},{6,8},{8,10},{10,12},{12,14},{1,3},{3,5},{5,7},{... | collective-permute-start | bytes 1572872 | tf_op jit(solution)/shard_map/ppermute | solution.py:15
  17.9 24.2 %collective-permute-start.2 = (bf16[512,512]{1,0:T(8,128)(2,1)}, bf16[512,512]{1,0:T(8,128)(2,1)}, u32[]{:S(2)}, u32[]{:S(2)}) collective-permute-start(bf16[512,512]{1,0:T(8,128)(2,1)} %param.7), channel_id=1, source_target_pairs={{2,0},{4,2},{6,4},{8,6},{10,8},{12,10},{14,12},{3,1},{5,3},{7,5},{... | collective-permute-start | bytes 1572872 | tf_op jit(solution)/shard_map/ppermute | solution.py:15
  19.2 28.4 %collective-permute-start.3 = (bf16[512,512]{1,0:T(8,128)(2,1)}, bf16[512,512]{1,0:T(8,128)(2,1)}, u32[]{:S(2)}, u32[]{:S(2)}) collective-permute-start(bf16[512,512]{1,0:T(8,128)(2,1)} %param.7), channel_id=1, source_target_pairs={{4,0},{6,2},{8,4},{10,6},{12,8},{14,10},{5,1},{7,3},{9,5},{11,7},{... | collective-permute-start | bytes 1572872 | tf_op jit(solution)/shard_map/ppermute | solution.py:15
  20.5 58.1 %all-gather.9.cloned.1.call-start = ((), (), s32[]{:S(2)}) async-start(), calls=%async_computation.3 | async-start | bytes 1572864 | tf_op jit(solution)/shard_map/all_gather | solution.py:40
  55.7 66.2 %all-gather.11.cloned.1.call-start = ((), (), s32[]{:S(2)}) async-start(), calls=%async_computation.4 | async-start | bytes 1179648 | tf_op jit(solution)/shard_map/all_gather | solution.py:46
  56.3 160.7 %reduce-scatter.2.cloned.1.call-start = ((), (), s32[]{:S(2)}) async-start(), calls=%async_computation.5 | async-start | bytes 4718592 | tf_op jit(solution)/shard_map/reduce_scatter | solution.py:54
  70.9 54.2 %copy-start.3 = (bf16[512,512]{1,0:T(8,128)(2,1)S(1)}, bf16[512,512]{1,0:T(8,128)(2,1)}, u32[]{:S(2)}) copy-start(bf16[512,512]{1,0:T(8,128)(2,1)} %param.13) | copy-start | bytes 1572868
  78.6 46.5 %copy-start.2 = (bf16[512,1024]{1,0:T(8,128)(2,1)S(1)}, bf16[512,1024]{1,0:T(8,128)(2,1)}, u32[]{:S(2)}) copy-start(bf16[512,1024]{1,0:T(8,128)(2,1)} %all-gather.9.cloned.1.call-done) | copy-start | bytes 3145732
  125.1 1.2 copy-start.1
Sparse Core Ops, SparseCore 0:
  9.6 11.7 all-gather.4
  23.4 45.1 all-gather.6
  70.8 7.7 all-gather.8
  80.6 41.3 all-gather.10
  129.9 87.0 reduce-scatter.1
where the time goes:
time: 227 us; the launch traced here: 226 us
  waiting for transfers between devices  172 us (76%)
  between operations  13.9 us (6%)
  starting transfers between devices  12.7 us (6%)
  matrix products  11.4 us (5%)
  local copies, waits for them, and re-layouts  9.24 us (4%)
  other arithmetic  6.54 us (3%)
    reduce_scatter x1, waiting for transfers between devices, local(): lax.psum_scatter(jnp.concatenate([jnp.einsum('nk,nh->kh', full_feat, grad...  87.2 us
    all_gather x1, waiting for transfers between devices, local(): lax.all_gather(w_neigh, 'rows', axis=0, tiled=True)  43.3 us
    ppermute x4, waiting for transfers between devices, passed_along(): return lax.ppermute(array, axis, pairs)  20.7 us
    ppermute x4, starting transfers between devices, passed_along(): return lax.ppermute(array, axis, pairs)  12.5 us
    all_gather x1, waiting for transfers between devices, local(): lax.all_gather(w_self, 'rows', axis=0, tiled=True)  12.3 us
    all_gather x1, waiting for transfers between devices, local(): full_agg = lax.all_gather(aggregated, 'cols', axis=1, tiled=True)  7.69 us
    dot_general x2, matrix products, add_rows(): return jnp.dot(left, piece, preferred_element_type=jnp.float32)  5.44 us
    unnamed x14, local copies, waits for them, and re-layouts  5.31 us
  transfers between devices with their start and end apart: 9, of which 7 were waited for; matrix products, arithmetic and copies ran while one was open for 7% of the time, Pallas kernels for 0%

commit v1 on v0

--- a/solution.py
+++ b/solution.py
@@ -1,12 +1,16 @@
+import functools
 import math
 
 import jax
 import jax.numpy as jnp
 from jax import lax
+from jax.experimental import pallas as pl
+from jax.experimental.pallas import tpu as pltpu
 from jax.sharding import PartitionSpec as P
 
 B = 128
 REACH = 2
+TILE = 128
 
 
 def passed_along(array, axis, by):
@@ -69,7 +73,334 @@
     return (output, grad_self, grad_neigh)
 
 
+F32 = jnp.float32
+BF16 = jnp.bfloat16
+
+
+def dest_order(step, pair, pairs):
+    above = pairs - 1 - pair
+    low = jnp.where(step < above, pairs - 1 - step, step - above)
+    high = jnp.where(step < pair, step, pairs - 1 - (step - pair))
+    return jnp.where(step == pairs - 1, pair, jnp.where(2 * pair < pairs, low, high))
+
+
+def layer(
+    n, f_ref, e_ref, cols_ref, count_ref, ws_ref, wn_ref, cot_ref,
+    out_ref, gs_ref, gn_ref,
+    ext, full, agg, masked, inv_deg, w, gp, part, xs, xr, zs, zr,
+    h_recv, h_x, h_z, h_relay, c_send, c_recv, w_recv, w_send,
+    x_send, x_recv, z_send, z_recv,
+):
+    batch, row, col = lax.axis_index("batch"), lax.axis_index("rows"), lax.axis_index("cols")
+    pairs = n // 2
+    pair, side = row // 2, row % 2
+    partner = row + 1 - 2 * side
+    nodes, width = out_ref.shape[0], f_ref.shape[2]
+    depth = ws_ref.shape[0]
+    blocks, slots = e_ref.shape[0], e_ref.shape[1]
+    half = blocks // 2
+    has_up, has_down = pair < pairs - 1, pair > 0
+    pending = []
+
+    def remote(src, dst, send, recv, to):
+        return pltpu.make_async_remote_copy(
+            src_ref=src, dst_ref=dst, send_sem=send, recv_sem=recv,
+            device_id=to, device_id_type=pl.DeviceIdType.MESH,
+        )
+
+    def send(cond, make):
+        if cond is None:
+            make().start()
+        else:
+            @pl.when(cond)
+            def _():
+                make().start()
+        pending.append((cond, make))
+
+    def arrived(dst, sem):
+        remote(dst, dst, sem, sem, {"cols": 1 - col}).wait_recv()
+
+    barrier = pltpu.get_barrier_semaphore()
+    mesh_id = pl.DeviceIdType.MESH
+    for to in ({"cols": 1 - col}, {"batch": 1 - batch}, {"rows": partner}):
+        pl.semaphore_signal(barrier, inc=1, device_id=to, device_id_type=mesh_id)
+
+    @pl.when(has_up)
+    def _():
+        pl.semaphore_signal(barrier, inc=1, device_id={"rows": row + 2}, device_id_type=mesh_id)
+
+    @pl.when(has_down)
+    def _():
+        pl.semaphore_signal(barrier, inc=1, device_id={"rows": row - 2}, device_id_type=mesh_id)
+
+    w[0, pl.ds(pl.multiple_of(row * depth, depth), depth), :] = ws_ref[...]
+    w[1, pl.ds(pl.multiple_of(row * depth, depth), depth), :] = wn_ref[...]
+    pl.semaphore_wait(barrier, 3 + has_up.astype(jnp.int32) + has_down.astype(jnp.int32))
+
+    def shard(which, origin):
+        return w.at[which, pl.ds(pl.multiple_of(origin * depth, depth), depth), :]
+
+    def send_w(cond, way, origin, to):
+        send(cond, lambda: remote(
+            shard(batch, origin), shard(batch, origin),
+            w_send.at[way, origin], w_recv.at[batch, origin], to))
+
+    up, down = {"rows": row + 2}, {"rows": row - 2}
+    send_w(has_up, 0, row, up)
+    send_w(has_down, 1, row, down)
+    send_w(None, 2, row, {"rows": partner})
+
+    def rows_of(slot, piece):
+        return ext.at[pl.ds(slot * blocks + piece * half, half)]
+
+    partner_slot = 3 - 2 * side
+    diag_slot = 1 + 2 * side
+    far_slot = 4 - 4 * side
+    for piece in (0, 1):
+        send(None, lambda piece=piece: remote(
+            f_ref.at[pl.ds(piece * half, half)], rows_of(diag_slot, piece),
+            h_x.at[piece], h_recv.at[diag_slot, piece], {"rows": partner}))
+        other = 1 - piece
+        send(has_up, lambda piece=other: remote(
+            f_ref.at[pl.ds(piece * half, half)], rows_of(0, piece),
+            h_z.at[0, piece], h_recv.at[0, piece], up))
+        send(has_down, lambda piece=other: remote(
+            f_ref.at[pl.ds(piece * half, half)], rows_of(4, piece),
+            h_z.at[1, piece], h_recv.at[4, piece], down))
+    send(None, lambda: remote(
+        f_ref, full.at[col], c_send.at[0], c_recv.at[0], {"cols": 1 - col}))
+
+    ext[REACH * blocks:(REACH + 1) * blocks] = f_ref[...]
+    full[col] = f_ref[...]
+
+    def prepare(i, carry):
+        degree = jnp.zeros((B, B), F32)
+        for s in range(slots):
+            keep = jnp.clip(count_ref[i] - s, 0, 1).astype(F32)
+            edge = e_ref[i, s].astype(F32) * keep
+            masked[i, :, s * B:(s + 1) * B] = edge.astype(BF16)
+            degree = degree + edge
+        total = jnp.sum(degree, axis=1, keepdims=True)
+        inv_deg[i] = jnp.broadcast_to(1.0 / total, (B, B))
+        return carry
+
+    lax.fori_loop(0, blocks, prepare, 0)
+
+    def forward(origin, cond, along, way, to):
+        @pl.when(cond)
+        def _():
+            arrived(shard(batch, origin), w_recv.at[batch, origin])
+        send_w(cond & along, way, origin, to)
+        send_w(cond, 2, origin, {"rows": partner})
+        send_w(cond, 3, origin, {"batch": 1 - batch})
+
+    def hand_over(origin, cond):
+        def wait():
+            arrived(shard(batch, origin), w_recv.at[batch, origin])
+        if cond is None:
+            wait()
+        else:
+            pl.when(cond)(wait)
+        send_w(cond, 3, origin, {"batch": 1 - batch})
+
+    has_far = jnp.where(side == 0, has_up.astype(jnp.int32), has_down.astype(jnp.int32)) == 1
+    has_diag = jnp.where(side == 0, has_down.astype(jnp.int32), has_up.astype(jnp.int32)) == 1
+    far = row + 2 - 4 * side
+    hand_over(partner, None)
+    for hop in range(1, pairs):
+        below, above = pair >= hop, pair + hop < pairs
+        forward(row - 2 * hop, below, has_up, 0, up)
+        forward(row + 2 * hop, above, has_down, 1, down)
+        if hop == 1:
+            arrived(rows_of(partner_slot, 0), h_recv.at[partner_slot, 0])
+            send(has_far, lambda: remote(
+                rows_of(partner_slot, 0), rows_of(diag_slot, 0),
+                h_relay.at[0], h_recv.at[diag_slot, 0], {"rows": far}))
+
+            @pl.when(has_far)
+            def _():
+                arrived(rows_of(far_slot, 1), h_recv.at[far_slot, 1])
+            send(has_far, lambda: remote(
+                rows_of(far_slot, 1), rows_of(partner_slot, 1),
+                h_relay.at[1], h_recv.at[partner_slot, 1], {"rows": partner}))
+        hand_over(partner - 2 * hop, below)
+        hand_over(partner + 2 * hop, above)
+
+    arrived(rows_of(partner_slot, 1), h_recv.at[partner_slot, 1])
+
+    @pl.when(has_far)
+    def _():
+        arrived(rows_of(far_slot, 0), h_recv.at[far_slot, 0])
+
+    @pl.when(has_diag)
+    def _():
+        for piece in (0, 1):
+            arrived(rows_of(4 - far_slot, piece), h_recv.at[4 - far_slot, piece])
+            arrived(rows_of(diag_slot, piece), h_recv.at[diag_slot, piece])
+
+    first = (row - REACH) * blocks
+
+    def aggregate(i, carry):
+        acc = jnp.zeros((B, width), F32)
+        for s in range(0, slots, 2):
+            picked = []
+            for k in (s, s + 1):
+                picked.append(ext[jnp.clip(cols_ref[i, k] - first, 0, ext.shape[0] - 1)])
+            acc = acc + jnp.dot(
+                masked[i, :, s * B:(s + 2) * B], jnp.concatenate(picked, axis=0),
+                preferred_element_type=F32)
+        agg[col, i] = (acc * inv_deg[i, :, 0:1]).astype(BF16)
+        return carry
+
+    lax.fori_loop(0, blocks, aggregate, 0)
+    send(None, lambda: remote(
+        agg.at[col], agg.at[col], c_send.at[1], c_recv.at[1], {"cols": 1 - col}))
+
+    arrived(full.at[1 - col], c_recv.at[0])
+
+    def handed_over(cond, origin):
+        def wait():
+            arrived(shard(1 - batch, origin), w_recv.at[1 - batch, origin])
+        if cond is None:
+            wait()
+        else:
+            pl.when(cond)(wait)
+
+    handed_over(None, partner)
+    for hop in range(1, pairs):
+        for origin in (row, partner):
+            handed_over(pair >= hop, origin - 2 * hop)
+            handed_over(pair + hop < pairs, origin + 2 * hop)
+    arrived(agg.at[1 - col], c_recv.at[1])
+
+    span = 2
+    tile = span * B
+
+    def left(array, h, i):
+        return array[h, pl.ds(i * span, span)].reshape(tile, width)
+
+    def activate(i, carry):
+        at = pl.ds(pl.multiple_of(i * tile, tile), tile)
+        pre = jnp.zeros((tile, w.shape[2]), F32)
+        for h in (0, 1):
+            pre = pre + jnp.dot(left(full, h, i), w[0, h * width:(h + 1) * width, :], preferred_element_type=F32)
+            pre = pre + jnp.dot(left(agg, h, i), w[1, h * width:(h + 1) * width, :], preferred_element_type=F32)
+        sigma = jax.nn.sigmoid(pre)
+        out_ref[at, :] = (pre * sigma).astype(BF16)
+        gp[at, :] = (cot_ref[at, :].astype(F32) * sigma * (1.0 + pre * (1.0 - sigma))).astype(BF16)
+        return carry
+
+    lax.fori_loop(0, nodes // tile, activate, 0)
+
+    per_half = width // depth
+
+    def gradient(array, chunk):
+        at = pl.ds(pl.multiple_of((chunk % per_half) * depth, depth), depth)
+        return lax.dot_general(
+            array[chunk // per_half, :, :, at].reshape(nodes, depth), gp[...], (((0,), (0,)), ((), ())),
+            preferred_element_type=F32)
+
+    dests = [dest_order(step, pair, pairs) for step in range(pairs)]
+    for step, dest in enumerate(dests):
+        chunk = 2 * dest + 1 - side
+        xs[step, :depth, :] = gradient(full, chunk).astype(BF16)
+        xs[step, depth:, :] = gradient(agg, chunk).astype(BF16)
+        send(None, lambda step=step: remote(
+            xs.at[step], xr.at[step], x_send.at[step], x_recv.at[step], {"rows": partner}))
+    for step, dest in enumerate(dests):
+        chunk = 2 * dest + side
+        part[step, :depth, :] = gradient(full, chunk)
+        part[step, depth:, :] = gradient(agg, chunk)
+    for step, dest in enumerate(dests):
+        arrived(xr.at[step], x_recv.at[step])
+        part[step] = part[step] + xr[step].astype(F32)
+        if step < pairs - 1:
+            way = jnp.where(dest > pair, 0, 1)
+            upstream = jnp.where(dest > pair, has_down.astype(jnp.int32), has_up.astype(jnp.int32)) == 1
+
+            @pl.when(upstream)
+            def _():
+                arrived(zr.at[way, dest], z_recv.at[way, dest])
+                part[step] = part[step] + zr[way, dest].astype(F32)
+
+            zs[step] = part[step].astype(BF16)
+            send(None, lambda step=step, way=way, dest=dest: remote(
+                zs.at[step], zr.at[way, dest], z_send.at[step], z_recv.at[way, dest],
+                {"rows": row + 2 - 4 * way}))
+        else:
+            for way, cond in ((0, has_down), (1, has_up)):
+                @pl.when(cond)
+                def _():
+                    arrived(zr.at[way, pair], z_recv.at[way, pair])
+                    part[step] = part[step] + zr[way, pair].astype(F32)
+            scale = 1.0 / math.sqrt(nodes * n)
+            gs_ref[...] = part[step, :depth, :] * scale
+            gn_ref[...] = part[step, depth:, :] * scale
+
+    for cond, make in pending:
+        if cond is None:
+            make().wait_send()
+        else:
+            @pl.when(cond)
+            def _():
+                make().wait_send()
+
+
+def fused(n, features, edge_vals, block_cols, block_count, w_self, w_neigh, cotangent):
+    nodes, width = features.shape
+    depth, out_cols = w_self.shape
+    blocks, slots = block_cols.shape
+    pairs = n // 2
+    dma = pltpu.SemaphoreType.DMA
+    vmem = pl.BlockSpec(memory_space=pltpu.VMEM)
+    smem = pl.BlockSpec(memory_space=pltpu.SMEM)
+    flops = 2 * nodes * width * (slots * B + 8 * out_cols)
+    return pl.pallas_call(
+        functools.partial(layer, n),
+        out_shape=(
+            jax.ShapeDtypeStruct((nodes, out_cols), BF16),
+            jax.ShapeDtypeStruct((depth, out_cols), F32),
+            jax.ShapeDtypeStruct((depth, out_cols), F32),
+        ),
+        in_specs=[vmem, vmem, smem, smem, vmem, vmem, vmem],
+        out_specs=(vmem, vmem, vmem),
+        scratch_shapes=[
+            pltpu.VMEM(((2 * REACH + 1) * blocks, B, width), BF16),
+            pltpu.VMEM((2, blocks, B, width), BF16),
+            pltpu.VMEM((2, blocks, B, width), BF16),
+            pltpu.VMEM((blocks, B, slots * B), BF16),
+            pltpu.VMEM((blocks, B, B), F32),
+            pltpu.VMEM((2, n * depth, out_cols), BF16),
+            pltpu.VMEM((nodes, out_cols), BF16),
+            pltpu.VMEM((pairs, 2 * depth, out_cols), F32),
+            pltpu.VMEM((pairs, 2 * depth, out_cols), BF16),
+            pltpu.VMEM((pairs, 2 * depth, out_cols), BF16),
+            pltpu.VMEM((pairs, 2 * depth, out_cols), BF16),
+            pltpu.VMEM((2, pairs, 2 * depth, out_cols), BF16),
+            dma((2 * REACH + 1, 2)), dma((2,)), dma((2, 2)), dma((2,)),
+            dma((2,)), dma((2,)), dma((2, n)), dma((4, n)),
+            dma((pairs,)), dma((pairs,)), dma((pairs,)), dma((2, pairs)),
+        ],
+        compiler_params=pltpu.CompilerParams(
+            collective_id=0, has_side_effects=True, vmem_limit_bytes=44 * 2**20,
+        ),
+        cost_estimate=pl.CostEstimate(
+            flops=flops, bytes_accessed=2 * edge_vals.size + 6 * features.size,
+            transcendentals=nodes * out_cols,
+        ),
+    )(features.reshape(blocks, B, width), edge_vals, block_cols, block_count, w_self, w_neigh, cotangent)
+
+
+def placed_layer(batches, n, cols, *arrays):
+    depth = arrays[4].shape[0]
+    width = arrays[0].shape[1]
+    if batches == 2 and cols == 2 and n % 2 == 0 and depth % TILE == 0 and width % depth == 0:
+        return fused(n, *arrays)
+    return local(*arrays)
+
+
 def solution(mesh):
+    body = functools.partial(placed_layer, mesh.shape["batch"], mesh.shape["rows"], mesh.shape["cols"])
     placed = (
         P(("batch", "rows"), "cols"),
         P(("batch", "rows"), None, None, None),
@@ -80,7 +411,7 @@
         P(("batch", "rows"), "cols"),
     )
     return jax.shard_map(
-        local,
+        body,
         mesh=mesh,
         in_specs=placed,
         out_specs=(

time: 227 us -> 81.7 us (0.36)
  the two profiles are of different devices: /device:TPU:0 before, /device:TPU:2 now
where the time goes in v1:
time: 81.7 us; the launch traced here: 81.4 us
  Pallas kernels  72.1 us (88%)
  local copies, waits for them, and re-layouts  8.64 us (11%)
    pallas_call x1, Pallas kernels, fused(): pl.pallas_call(functools.partial(layer, n), out_shape=(jax.ShapeDtypeStru...  72.1 us
    unnamed x17, local copies, waits for them, and re-layouts  8.64 us

profile of v1, /device:TPU:2, one launch (start us, length us, event | category | flops | bytes accessed | tf_op | source)
XLA Modules:
  0.0 81.4 jit_solution(1305482823613258515)
XLA Ops:
  0.6 0.0 copy-start.6
  0.6 0.6 copy-done.6
  1.3 0.0 copy-start
  1.3 1.2 %copy-done = bf16[4,8,128,128]{3,2,1,0:T(8,128)(2,1)S(1)} copy-done((bf16[4,8,128,128]{3,2,1,0:T(8,128)(2,1)S(1)}, bf16[4,8,128,128]{3,2,1,0:T(8,128)(2,1)}, u32[]{:S(2)}) %copy-start) | copy-done | bytes 1048600
  2.5 0.0 copy-start.1
  2.5 1.0 %copy-done.1 = bf16[512,512]{1,0:T(8,128)(2,1)S(1)} copy-done((bf16[512,512]{1,0:T(8,128)(2,1)S(1)}, bf16[512,512]{1,0:T(8,128)(2,1)}, u32[]{:S(2)}) %copy-start.1) | copy-done | bytes 524312
  3.6 0.0 copy-start.2
  3.6 1.0 %copy-done.2 = bf16[512,512]{1,0:T(8,128)(2,1)S(1)} copy-done((bf16[512,512]{1,0:T(8,128)(2,1)S(1)}, bf16[512,512]{1,0:T(8,128)(2,1)}, u32[]{:S(2)}) %copy-start.2) | copy-done | bytes 524312
  4.6 0.0 copy-start.3
  4.6 0.9 %copy-done.3 = bf16[128,512]{1,0:T(8,128)(2,1)S(1)} copy-done((bf16[128,512]{1,0:T(8,128)(2,1)S(1)}, bf16[128,512]{1,0:T(8,128)(2,1)}, u32[]{:S(2)}) %copy-start.3) | copy-done | bytes 131096
  5.5 0.0 copy-start.4
  5.5 0.9 %copy-done.4 = bf16[128,512]{1,0:T(8,128)(2,1)S(1)} copy-done((bf16[128,512]{1,0:T(8,128)(2,1)S(1)}, bf16[128,512]{1,0:T(8,128)(2,1)}, u32[]{:S(2)}) %copy-start.4) | copy-done | bytes 131096
  6.4 0.0 copy-start.5
  6.4 0.7 copy-done.5
  7.1 72.1 %shard_map.94 = (bf16[512,512]{1,0:T(8,128)(2,1)S(1)}, f32[128,512]{1,0:T(8,128)S(1)}, f32[128,512]{1,0:T(8,128)S(1)}) custom-call(bf16[4,128,512]{2,1,0:T(8,128)(2,1)S(1)} %bitcast.1, bf16[4,8,128,128]{3,2,1,0:T(8,128)(2,1)S(1)} %copy-done, s32[4,8]{1,0:T(4,128)S(1)} %copy-done.5, s32[4]{0:T(128)S(1)} %copy-done.6, bf16[128,512]{1,0:T(8,128)(2,1)S(1)} %copy-done.3, ...), custom_call_target="tpu_custom_call" | custom-call | flops 2684354560 | bytes 2621440 | tf_op jit(solution)/shard_map/pallas_call | solution.py:358
  79.2 0.8 copy.13
  80.0 0.7 copy.14
  80.7 0.7 copy.15
Async XLA Ops:
  0.6 0.7 copy-start.6
  1.3 1.2 %copy-start = (bf16[4,8,128,128]{3,2,1,0:T(8,128)(2,1)S(1)}, bf16[4,8,128,128]{3,2,1,0:T(8,128)(2,1)}, u32[]{:S(2)}) copy-start(bf16[4,8,128,128]{3,2,1,0:T(8,128)(2,1)} %e_ref.1) | copy-start | bytes 3145732
  2.5 1.0 %copy-start.1 = (bf16[512,512]{1,0:T(8,128)(2,1)S(1)}, bf16[512,512]{1,0:T(8,128)(2,1)}, u32[]{:S(2)}) copy-start(bf16[512,512]{1,0:T(8,128)(2,1)} %param.7) | copy-start | bytes 1572868
  3.6 1.0 %copy-start.2 = (bf16[512,512]{1,0:T(8,128)(2,1)S(1)}, bf16[512,512]{1,0:T(8,128)(2,1)}, u32[]{:S(2)}) copy-start(bf16[512,512]{1,0:T(8,128)(2,1)} %cot_ref.1) | copy-start | bytes 1572868
  4.6 0.9 %copy-start.3 = (bf16[128,512]{1,0:T(8,128)(2,1)S(1)}, bf16[128,512]{1,0:T(8,128)(2,1)}, u32[]{:S(2)}) copy-start(bf16[128,512]{1,0:T(8,128)(2,1)} %ws_ref.1) | copy-start | bytes 393220
  5.5 0.9 %copy-start.4 = (bf16[128,512]{1,0:T(8,128)(2,1)S(1)}, bf16[128,512]{1,0:T(8,128)(2,1)}, u32[]{:S(2)}) copy-start(bf16[128,512]{1,0:T(8,128)(2,1)} %wn_ref.1) | copy-start | bytes 393220
  6.4 0.7 copy-start.5

commit v2 on v1

--- a/solution.py
+++ b/solution.py
@@ -85,18 +85,18 @@
 
 
 def layer(
-    n, f_ref, e_ref, cols_ref, count_ref, ws_ref, wn_ref, cot_ref,
-    out_ref, gs_ref, gn_ref,
+    n, f_hbm, e_hbm, cols_ref, count_ref, ws_hbm, wn_hbm, cot_hbm,
+    out_hbm, grad_ref, e_ref, cot_ref, out_ref,
     ext, full, agg, masked, inv_deg, w, gp, part, xs, xr, zs, zr,
-    h_recv, h_x, h_z, h_relay, c_send, c_recv, w_recv, w_send,
+    h_recv, h_x, h_z, h_relay, c_send, c_recv, w_recv, w_send, w_far, here,
     x_send, x_recv, z_send, z_recv,
 ):
     batch, row, col = lax.axis_index("batch"), lax.axis_index("rows"), lax.axis_index("cols")
     pairs = n // 2
     pair, side = row // 2, row % 2
     partner = row + 1 - 2 * side
-    nodes, width = out_ref.shape[0], f_ref.shape[2]
-    depth = ws_ref.shape[0]
+    nodes, width = out_ref.shape[0], f_hbm.shape[2]
+    depth = ws_hbm.shape[0]
     blocks, slots = e_ref.shape[0], e_ref.shape[1]
     half = blocks // 2
     has_up, has_down = pair < pairs - 1, pair > 0
@@ -120,35 +120,38 @@
     def arrived(dst, sem):
         remote(dst, dst, sem, sem, {"cols": 1 - col}).wait_recv()
 
-    barrier = pltpu.get_barrier_semaphore()
-    mesh_id = pl.DeviceIdType.MESH
-    for to in ({"cols": 1 - col}, {"batch": 1 - batch}, {"rows": partner}):
-        pl.semaphore_signal(barrier, inc=1, device_id=to, device_id_type=mesh_id)
-
-    @pl.when(has_up)
-    def _():
-        pl.semaphore_signal(barrier, inc=1, device_id={"rows": row + 2}, device_id_type=mesh_id)
-
-    @pl.when(has_down)
-    def _():
-        pl.semaphore_signal(barrier, inc=1, device_id={"rows": row - 2}, device_id_type=mesh_id)
-
-    w[0, pl.ds(pl.multiple_of(row * depth, depth), depth), :] = ws_ref[...]
-    w[1, pl.ds(pl.multiple_of(row * depth, depth), depth), :] = wn_ref[...]
-    pl.semaphore_wait(barrier, 3 + has_up.astype(jnp.int32) + has_down.astype(jnp.int32))
-
     def shard(which, origin):
         return w.at[which, pl.ds(pl.multiple_of(origin * depth, depth), depth), :]
 
-    def send_w(cond, way, origin, to):
+    own = ext.at[pl.ds(REACH * blocks, blocks)]
+    loads = [
+        pltpu.make_async_copy(src, dst, here.at[k])
+        for k, (src, dst) in enumerate((
+            (ws_hbm, shard(0, row)), (wn_hbm, shard(1, row)), (f_hbm, own),
+            (e_hbm, e_ref), (f_hbm, full.at[col]), (cot_hbm, cot_ref),
+        ))
+    ]
+    for load in loads:
+        load.start()
+
+    barrier = pltpu.get_barrier_semaphore()
+    greeted = [{"cols": 1 - col}, {"batch": 1 - batch}, {"rows": partner}]
+    greeted += [{"rows": (row + 2 * hop) % n} for hop in range(1, pairs)]
+    for to in greeted:
+        pl.semaphore_signal(barrier, inc=1, device_id=to, device_id_type=pl.DeviceIdType.MESH)
+    for load in loads[:3]:
+        load.wait()
+    pl.semaphore_wait(barrier, len(greeted))
+
+    def send_w(cond, sem, origin, to):
         send(cond, lambda: remote(
-            shard(batch, origin), shard(batch, origin),
-            w_send.at[way, origin], w_recv.at[batch, origin], to))
+            shard(batch, origin), shard(batch, origin), sem, w_recv.at[batch, origin], to))
 
     up, down = {"rows": row + 2}, {"rows": row - 2}
-    send_w(has_up, 0, row, up)
-    send_w(has_down, 1, row, down)
-    send_w(None, 2, row, {"rows": partner})
+    for hop in range(1, pairs):
+        send_w(pair + hop < pairs, w_far.at[0, hop], row, {"rows": row + 2 * hop})
+        send_w(pair >= hop, w_far.at[1, hop], row, {"rows": row - 2 * hop})
+    send_w(None, w_send.at[0, row], row, {"rows": partner})
 
     def rows_of(slot, piece):
         return ext.at[pl.ds(slot * blocks + piece * half, half)]
@@ -158,20 +161,19 @@
     far_slot = 4 - 4 * side
     for piece in (0, 1):
         send(None, lambda piece=piece: remote(
-            f_ref.at[pl.ds(piece * half, half)], rows_of(diag_slot, piece),
+            rows_of(REACH, piece), rows_of(diag_slot, piece),
             h_x.at[piece], h_recv.at[diag_slot, piece], {"rows": partner}))
         other = 1 - piece
         send(has_up, lambda piece=other: remote(
-            f_ref.at[pl.ds(piece * half, half)], rows_of(0, piece),
+            rows_of(REACH, piece), rows_of(0, piece),
             h_z.at[0, piece], h_recv.at[0, piece], up))
         send(has_down, lambda piece=other: remote(
-            f_ref.at[pl.ds(piece * half, half)], rows_of(4, piece),
+            rows_of(REACH, piece), rows_of(4, piece),
             h_z.at[1, piece], h_recv.at[4, piece], down))
     send(None, lambda: remote(
-        f_ref, full.at[col], c_send.at[0], c_recv.at[0], {"cols": 1 - col}))
-
-    ext[REACH * blocks:(REACH + 1) * blocks] = f_ref[...]
-    full[col] = f_ref[...]
+        own, full.at[col], c_send.at[0], c_recv.at[0], {"cols": 1 - col}))
+
+    loads[3].wait()
 
     def prepare(i, carry):
         degree = jnp.zeros((B, B), F32)
@@ -186,13 +188,12 @@
 
     lax.fori_loop(0, blocks, prepare, 0)
 
-    def forward(origin, cond, along, way, to):
+    def forward(origin, cond):
         @pl.when(cond)
         def _():
             arrived(shard(batch, origin), w_recv.at[batch, origin])
-        send_w(cond & along, way, origin, to)
-        send_w(cond, 2, origin, {"rows": partner})
-        send_w(cond, 3, origin, {"batch": 1 - batch})
+        send_w(cond, w_send.at[0, origin], origin, {"rows": partner})
+        send_w(cond, w_send.at[1, origin], origin, {"batch": 1 - batch})
 
     def hand_over(origin, cond):
         def wait():
@@ -201,30 +202,30 @@
             wait()
         else:
             pl.when(cond)(wait)
-        send_w(cond, 3, origin, {"batch": 1 - batch})
+        send_w(cond, w_send.at[1, origin], origin, {"batch": 1 - batch})
 
     has_far = jnp.where(side == 0, has_up.astype(jnp.int32), has_down.astype(jnp.int32)) == 1
     has_diag = jnp.where(side == 0, has_down.astype(jnp.int32), has_up.astype(jnp.int32)) == 1
     far = row + 2 - 4 * side
-    hand_over(partner, None)
     for hop in range(1, pairs):
-        below, above = pair >= hop, pair + hop < pairs
-        forward(row - 2 * hop, below, has_up, 0, up)
-        forward(row + 2 * hop, above, has_down, 1, down)
+        forward(row - 2 * hop, pair >= hop)
+        forward(row + 2 * hop, pair + hop < pairs)
         if hop == 1:
-            arrived(rows_of(partner_slot, 0), h_recv.at[partner_slot, 0])
-            send(has_far, lambda: remote(
-                rows_of(partner_slot, 0), rows_of(diag_slot, 0),
-                h_relay.at[0], h_recv.at[diag_slot, 0], {"rows": far}))
-
-            @pl.when(has_far)
-            def _():
-                arrived(rows_of(far_slot, 1), h_recv.at[far_slot, 1])
-            send(has_far, lambda: remote(
-                rows_of(far_slot, 1), rows_of(partner_slot, 1),
-                h_relay.at[1], h_recv.at[partner_slot, 1], {"rows": partner}))
-        hand_over(partner - 2 * hop, below)
-        hand_over(partner + 2 * hop, above)
+            hand_over(partner, None)
+    arrived(rows_of(partner_slot, 0), h_recv.at[partner_slot, 0])
+    send(has_far, lambda: remote(
+        rows_of(partner_slot, 0), rows_of(diag_slot, 0),
+        h_relay.at[0], h_recv.at[diag_slot, 0], {"rows": far}))
+
+    @pl.when(has_far)
+    def _():
+        arrived(rows_of(far_slot, 1), h_recv.at[far_slot, 1])
+    send(has_far, lambda: remote(
+        rows_of(far_slot, 1), rows_of(partner_slot, 1),
+        h_relay.at[1], h_recv.at[partner_slot, 1], {"rows": partner}))
+    for hop in range(1, pairs):
+        hand_over(partner - 2 * hop, pair >= hop)
+        hand_over(partner + 2 * hop, pair + hop < pairs)
 
     arrived(rows_of(partner_slot, 1), h_recv.at[partner_slot, 1])
 
@@ -275,6 +276,8 @@
 
     span = 2
     tile = span * B
+    for load in loads[4:]:
+        load.wait()
 
     def left(array, h, i):
         return array[h, pl.ds(i * span, span)].reshape(tile, width)
@@ -291,6 +294,8 @@
         return carry
 
     lax.fori_loop(0, nodes // tile, activate, 0)
+    store = pltpu.make_async_copy(out_ref, out_hbm, here.at[len(loads)])
+    store.start()
 
     per_half = width // depth
 
@@ -333,9 +338,8 @@
                 def _():
                     arrived(zr.at[way, pair], z_recv.at[way, pair])
                     part[step] = part[step] + zr[way, pair].astype(F32)
-            scale = 1.0 / math.sqrt(nodes * n)
-            gs_ref[...] = part[step, :depth, :] * scale
-            gn_ref[...] = part[step, depth:, :] * scale
+            grad_ref[...] = part[step]
+    store.wait()
 
     for cond, make in pending:
         if cond is None:
@@ -353,18 +357,21 @@
     pairs = n // 2
     dma = pltpu.SemaphoreType.DMA
     vmem = pl.BlockSpec(memory_space=pltpu.VMEM)
+    hbm = pl.BlockSpec(memory_space=pltpu.HBM)
     smem = pl.BlockSpec(memory_space=pltpu.SMEM)
     flops = 2 * nodes * width * (slots * B + 8 * out_cols)
-    return pl.pallas_call(
+    output, total = pl.pallas_call(
         functools.partial(layer, n),
         out_shape=(
             jax.ShapeDtypeStruct((nodes, out_cols), BF16),
-            jax.ShapeDtypeStruct((depth, out_cols), F32),
-            jax.ShapeDtypeStruct((depth, out_cols), F32),
+            jax.ShapeDtypeStruct((2 * depth, out_cols), F32),
         ),
-        in_specs=[vmem, vmem, smem, smem, vmem, vmem, vmem],
-        out_specs=(vmem, vmem, vmem),
+        in_specs=[hbm, hbm, smem, smem, hbm, hbm, hbm],
+        out_specs=(hbm, vmem),
         scratch_shapes=[
+            pltpu.VMEM(edge_vals.shape, BF16),
+            pltpu.VMEM((nodes, out_cols), BF16),
+            pltpu.VMEM((nodes, out_cols), BF16),
             pltpu.VMEM(((2 * REACH + 1) * blocks, B, width), BF16),
             pltpu.VMEM((2, blocks, B, width), BF16),
             pltpu.VMEM((2, blocks, B, width), BF16),
@@ -378,7 +385,7 @@
             pltpu.VMEM((pairs, 2 * depth, out_cols), BF16),
             pltpu.VMEM((2, pairs, 2 * depth, out_cols), BF16),
             dma((2 * REACH + 1, 2)), dma((2,)), dma((2, 2)), dma((2,)),
-            dma((2,)), dma((2,)), dma((2, n)), dma((4, n)),
+            dma((2,)), dma((2,)), dma((2, n)), dma((2, n)), dma((2, pairs)), dma((7,)),
             dma((pairs,)), dma((pairs,)), dma((pairs,)), dma((2, pairs)),
         ],
         compiler_params=pltpu.CompilerParams(
@@ -389,6 +396,8 @@
             transcendentals=nodes * out_cols,
         ),
     )(features.reshape(blocks, B, width), edge_vals, block_cols, block_count, w_self, w_neigh, cotangent)
+    scaled = total * (1.0 / math.sqrt(nodes * n))
+    return output, scaled[:depth], scaled[depth:]
 
 
 def placed_layer(batches, n, cols, *arrays):

time: 81.7 us -> 78.4 us (0.960)
  the two profiles are of different devices: /device:TPU:2 before, /device:TPU:0 now
where the time goes in v2:
time: 78.4 us; the launch traced here: 78 us
  Pallas kernels  69.3 us (88%)
  local copies, waits for them, and re-layouts  8.06 us (10%)
    pallas_call x1, Pallas kernels, fused(): pl.pallas_call(functools.partial(layer, n), out_shape=(jax.ShapeDtypeStru...  69.3 us
    unnamed x15, local copies, waits for them, and re-layouts  7.24 us

profile of v2, /device:TPU:0, one launch (start us, length us, event | category | flops | bytes accessed | tf_op | source)
XLA Modules:
  0.0 78.0 jit_solution(17517905732858063156)
XLA Ops:
  0.6 0.0 copy-start.6
  0.6 0.6 copy-done.6
  1.3 0.0 copy-start
  1.3 1.2 %copy-done = bf16[4,8,128,128]{3,2,1,0:T(8,128)(2,1)S(1)} copy-done((bf16[4,8,128,128]{3,2,1,0:T(8,128)(2,1)S(1)}, bf16[4,8,128,128]{3,2,1,0:T(8,128)(2,1)}, u32[]{:S(2)}) %copy-start) | copy-done | bytes 1048600
  2.5 0.0 copy-start.1
  2.5 1.0 %copy-done.1 = bf16[512,512]{1,0:T(8,128)(2,1)S(1)} copy-done((bf16[512,512]{1,0:T(8,128)(2,1)S(1)}, bf16[512,512]{1,0:T(8,128)(2,1)}, u32[]{:S(2)}) %copy-start.1) | copy-done | bytes 524312
  3.6 0.0 copy-start.2
  3.6 1.0 %copy-done.2 = bf16[512,512]{1,0:T(8,128)(2,1)S(1)} copy-done((bf16[512,512]{1,0:T(8,128)(2,1)S(1)}, bf16[512,512]{1,0:T(8,128)(2,1)}, u32[]{:S(2)}) %copy-start.2) | copy-done | bytes 524312
  4.6 0.0 copy-start.3
  4.6 0.9 %copy-done.3 = bf16[128,512]{1,0:T(8,128)(2,1)S(1)} copy-done((bf16[128,512]{1,0:T(8,128)(2,1)S(1)}, bf16[128,512]{1,0:T(8,128)(2,1)}, u32[]{:S(2)}) %copy-start.3) | copy-done | bytes 131096
  5.5 0.0 copy-start.4
  5.5 0.9 %copy-done.4 = bf16[128,512]{1,0:T(8,128)(2,1)S(1)} copy-done((bf16[128,512]{1,0:T(8,128)(2,1)S(1)}, bf16[128,512]{1,0:T(8,128)(2,1)}, u32[]{:S(2)}) %copy-start.4) | copy-done | bytes 131096
  6.4 0.0 copy-start.5
  6.4 0.7 copy-done.5
  7.1 69.3 %shard_map.94 = (bf16[512,512]{1,0:T(8,128)(2,1)S(1)}, f32[256,512]{1,0:T(8,128)S(1)}) custom-call(bf16[4,128,512]{2,1,0:T(8,128)(2,1)S(1)} %bitcast.1, bf16[4,8,128,128]{3,2,1,0:T(8,128)(2,1)S(1)} %copy-done, s32[4,8]{1,0:T(4,128)S(1)} %copy-done.5, s32[4]{0:T(128)S(1)} %copy-done.6, bf16[128,512]{1,0:T(8,128)(2,1)S(1)} %copy-done.3, ...), custom_call_target="tpu_custom_call" | custom-call | flops 2684354560 | bytes 2621440 | tf_op jit(solution)/shard_map/pallas_call | solution.py:363
  76.4 0.8 %fusion = (f32[128,512]{1,0:T(8,128)}, f32[128,512]{1,0:T(8,128)}) fusion(f32[256,512]{1,0:T(8,128)S(1)} %broadcast_multiply_fusion), kind=kLoop, calls=%fused_computation.1 | loop fusion | bytes 1048576 | tf_op jit(solution)/shard_map/slice | solution.py:400
  77.2 0.8 %copy.11 = bf16[512,512]{1,0:T(8,128)(2,1)} copy(bf16[512,512]{1,0:T(8,128)(2,1)S(1)} %get-tuple-element.12) | data formatting | bytes 1048576
  (1 shorter events, 0.0 us)
Async XLA Ops:
  0.6 0.7 copy-start.6
  1.3 1.2 %copy-start = (bf16[4,8,128,128]{3,2,1,0:T(8,128)(2,1)S(1)}, bf16[4,8,128,128]{3,2,1,0:T(8,128)(2,1)}, u32[]{:S(2)}) copy-start(bf16[4,8,128,128]{3,2,1,0:T(8,128)(2,1)} %e_hbm.1) | copy-start | bytes 3145732
  2.5 1.0 %copy-start.1 = (bf16[512,512]{1,0:T(8,128)(2,1)S(1)}, bf16[512,512]{1,0:T(8,128)(2,1)}, u32[]{:S(2)}) copy-start(bf16[512,512]{1,0:T(8,128)(2,1)} %param.7) | copy-start | bytes 1572868
  3.6 1.0 %copy-start.2 = (bf16[512,512]{1,0:T(8,128)(2,1)S(1)}, bf16[512,512]{1,0:T(8,128)(2,1)}, u32[]{:S(2)}) copy-start(bf16[512,512]{1,0:T(8,128)(2,1)} %cot_hbm.1) | copy-start | bytes 1572868
  4.6 0.9 %copy-start.3 = (bf16[128,512]{1,0:T(8,128)(2,1)S(1)}, bf16[128,512]{1,0:T(8,128)(2,1)}, u32[]{:S(2)}) copy-start(bf16[128,512]{1,0:T(8,128)(2,1)} %ws_hbm.1) | copy-start | bytes 393220
  5.5 0.9 %copy-start.4 = (bf16[128,512]{1,0:T(8,128)(2,1)S(1)}, bf16[128,512]{1,0:T(8,128)(2,1)}, u32[]{:S(2)}) copy-start(bf16[128,512]{1,0:T(8,128)(2,1)} %wn_hbm.1) | copy-start | bytes 393220
  6.4 0.7 copy-start.5

commit v3 on v2

--- a/solution.py
+++ b/solution.py
@@ -159,15 +159,18 @@
     partner_slot = 3 - 2 * side
     diag_slot = 1 + 2 * side
     far_slot = 4 - 4 * side
-    for piece in (0, 1):
-        send(None, lambda piece=piece: remote(
+
+    def send_x(piece):
+        send(None, lambda: remote(
             rows_of(REACH, piece), rows_of(diag_slot, piece),
             h_x.at[piece], h_recv.at[diag_slot, piece], {"rows": partner}))
-        other = 1 - piece
-        send(has_up, lambda piece=other: remote(
+
+    send_x(0)
+    for piece in (1, 0):
+        send(has_up, lambda piece=piece: remote(
             rows_of(REACH, piece), rows_of(0, piece),
             h_z.at[0, piece], h_recv.at[0, piece], up))
-        send(has_down, lambda piece=other: remote(
+        send(has_down, lambda piece=piece: remote(
             rows_of(REACH, piece), rows_of(4, piece),
             h_z.at[1, piece], h_recv.at[4, piece], down))
     send(None, lambda: remote(
@@ -212,6 +215,7 @@
         forward(row + 2 * hop, pair + hop < pairs)
         if hop == 1:
             hand_over(partner, None)
+    send_x(1)
     arrived(rows_of(partner_slot, 0), h_recv.at[partner_slot, 0])
     send(has_far, lambda: remote(
         rows_of(partner_slot, 0), rows_of(diag_slot, 0),
@@ -389,15 +393,15 @@
             dma((pairs,)), dma((pairs,)), dma((pairs,)), dma((2, pairs)),
         ],
         compiler_params=pltpu.CompilerParams(
-            collective_id=0, has_side_effects=True, vmem_limit_bytes=44 * 2**20,
+            collective_id=0, has_side_effects=True, vmem_limit_bytes=63 * 2**20,
         ),
         cost_estimate=pl.CostEstimate(
             flops=flops, bytes_accessed=2 * edge_vals.size + 6 * features.size,
             transcendentals=nodes * out_cols,
         ),
     )(features.reshape(blocks, B, width), edge_vals, block_cols, block_count, w_self, w_neigh, cotangent)
-    scaled = total * (1.0 / math.sqrt(nodes * n))
-    return output, scaled[:depth], scaled[depth:]
+    scale = 1.0 / math.sqrt(nodes * n)
+    return output, total[:depth] * scale, total[depth:] * scale
 
 
 def placed_layer(batches, n, cols, *arrays):

time: 78.4 us -> 71.8 us (0.916)
  local copies, waits for them, and re-layouts: 8.06 us -> 0.8 us
  other arithmetic: 0.04 us -> 1.92 us
  Pallas kernels: 69.3 us -> 68.2 us
    unnamed x15 -> x3, local copies, waits for them, and re-layouts: 7.24 us -> 0.8 us
    mul x1, other arithmetic: 0.04 us -> 1.92 us  [fused(): return (output, total[:depth] * scale, total[depth:] * scale)]
    pallas_call x1, Pallas kernels: 69.3 us -> 68.2 us  [fused(): pl.pallas_call(functools.partial(layer, n), out_shape=(jax.ShapeDtypeStru...]
    slice x1 -> x0, local copies, waits for them, and re-layouts: 0.83 us -> none  [fused(): return (output, scaled[:depth], scaled[depth:])]
where the time goes in v3:
time: 71.8 us; the launch traced here: 71.6 us
  Pallas kernels  68.2 us (95%)
  other arithmetic  1.92 us (3%)
  local copies, waits for them, and re-layouts  0.8 us (1%)
    pallas_call x1, Pallas kernels, fused(): pl.pallas_call(functools.partial(layer, n), out_shape=(jax.ShapeDtypeStru...  68.2 us
    mul x1, other arithmetic, fused(): return (output, total[:depth] * scale, total[depth:] * scale)  1.92 us

profile of v3, /device:TPU:0, one launch (start us, length us, event | category | flops | bytes accessed | tf_op | source)
XLA Modules:
  0.0 71.6 jit_solution(4429792835813704079)
XLA Ops:
  0.6 68.2 %shard_map.94 = (bf16[512,512]{1,0:T(8,128)(2,1)}, f32[256,512]{1,0:T(8,128)}) custom-call(bf16[4,128,512]{2,1,0:T(8,128)(2,1)} %bitcast.1, bf16[4,8,128,128]{3,2,1,0:T(8,128)(2,1)} %e_hbm.1, s32[4,8]{1,0:T(4,128)} %cols_ref.1, s32[4]{0:T(128)} %count_ref.1, bf16[128,512]{1,0:T(8,128)(2,1)} %ws_hbm.1, bf16[128,512]{1,0:T(8,128)(2,1)} %wn_hbm.1, ...), custom_call_target="tpu_custom_call" | custom-call | flops 2684354560 | bytes 2621440 | tf_op jit(solution)/shard_map/pallas_call | solution.py:367
  68.9 0.0 copy-start
  68.9 1.9 %slice_multiply_fusion = (f32[128,512]{1,0:T(8,128)}, f32[128,512]{1,0:T(8,128)}) fusion(f32[256,512]{1,0:T(8,128)} %get-tuple-element.6), kind=kLoop, calls=%fused_computation | loop fusion | flops 131072 | bytes 1048576 | tf_op jit(solution)/shard_map/mul | solution.py:404
  70.8 0.0 copy-done
  70.8 0.8 %copy.11 = bf16[512,512]{1,0:T(8,128)(2,1)} copy(bf16[512,512]{1,0:T(8,128)(2,1)S(1)} %copy-done) | data formatting | bytes 1048576
Async XLA Ops:
  68.9 1.9 %copy-start = (bf16[512,512]{1,0:T(8,128)(2,1)S(1)}, bf16[512,512]{1,0:T(8,128)(2,1)}, u32[]{:S(2)}) copy-start(bf16[512,512]{1,0:T(8,128)(2,1)} %get-tuple-element.12) | copy-start | bytes 1572868

commit v4 on v3

--- a/solution.py
+++ b/solution.py
@@ -310,39 +310,37 @@
             preferred_element_type=F32)
 
     dests = [dest_order(step, pair, pairs) for step in range(pairs)]
-    for step, dest in enumerate(dests):
-        chunk = 2 * dest + 1 - side
-        xs[step, :depth, :] = gradient(full, chunk).astype(BF16)
-        xs[step, depth:, :] = gradient(agg, chunk).astype(BF16)
-        send(None, lambda step=step: remote(
-            xs.at[step], xr.at[step], x_send.at[step], x_recv.at[step], {"rows": partner}))
-    for step, dest in enumerate(dests):
-        chunk = 2 * dest + side
-        part[step, :depth, :] = gradient(full, chunk)
-        part[step, depth:, :] = gradient(agg, chunk)
-    for step, dest in enumerate(dests):
-        arrived(xr.at[step], x_recv.at[step])
-        part[step] = part[step] + xr[step].astype(F32)
+    terms = [(step, dest, k) for step, dest in enumerate(dests) for k in (0, 1)]
+    for step, dest, k in terms:
+        xs[step, k] = gradient((full, agg)[k], 2 * dest + 1 - side).astype(BF16)
+        send(None, lambda step=step, k=k: remote(
+            xs.at[step, k], xr.at[step, k], x_send.at[step, k], x_recv.at[step, k],
+            {"rows": partner}))
+    for step, dest, k in terms:
+        part[step, k] = gradient((full, agg)[k], 2 * dest + side)
+    for step, dest, k in terms:
+        arrived(xr.at[step, k], x_recv.at[step, k])
+        part[step, k] = part[step, k] + xr[step, k].astype(F32)
         if step < pairs - 1:
             way = jnp.where(dest > pair, 0, 1)
             upstream = jnp.where(dest > pair, has_down.astype(jnp.int32), has_up.astype(jnp.int32)) == 1
 
             @pl.when(upstream)
             def _():
-                arrived(zr.at[way, dest], z_recv.at[way, dest])
-                part[step] = part[step] + zr[way, dest].astype(F32)
-
-            zs[step] = part[step].astype(BF16)
-            send(None, lambda step=step, way=way, dest=dest: remote(
-                zs.at[step], zr.at[way, dest], z_send.at[step], z_recv.at[way, dest],
+                arrived(zr.at[way, dest, k], z_recv.at[way, dest, k])
+                part[step, k] = part[step, k] + zr[way, dest, k].astype(F32)
+
+            zs[step, k] = part[step, k].astype(BF16)
+            send(None, lambda step=step, way=way, dest=dest, k=k: remote(
+                zs.at[step, k], zr.at[way, dest, k], z_send.at[step, k], z_recv.at[way, dest, k],
                 {"rows": row + 2 - 4 * way}))
         else:
             for way, cond in ((0, has_down), (1, has_up)):
                 @pl.when(cond)
                 def _():
-                    arrived(zr.at[way, pair], z_recv.at[way, pair])
-                    part[step] = part[step] + zr[way, pair].astype(F32)
-            grad_ref[...] = part[step]
+                    arrived(zr.at[way, pair, k], z_recv.at[way, pair, k])
+                    part[step, k] = part[step, k] + zr[way, pair, k].astype(F32)
+            grad_ref[k * depth:(k + 1) * depth, :] = part[step, k]
     store.wait()
 
     for cond, make in pending:
@@ -383,14 +381,14 @@
             pltpu.VMEM((blocks, B, B), F32),
             pltpu.VMEM((2, n * depth, out_cols), BF16),
             pltpu.VMEM((nodes, out_cols), BF16),
-            pltpu.VMEM((pairs, 2 * depth, out_cols), F32),
-            pltpu.VMEM((pairs, 2 * depth, out_cols), BF16),
-            pltpu.VMEM((pairs, 2 * depth, out_cols), BF16),
-            pltpu.VMEM((pairs, 2 * depth, out_cols), BF16),
-            pltpu.VMEM((2, pairs, 2 * depth, out_cols), BF16),
+            pltpu.VMEM((pairs, 2, depth, out_cols), F32),
+            pltpu.VMEM((pairs, 2, depth, out_cols), BF16),
+            pltpu.VMEM((pairs, 2, depth, out_cols), BF16),
+            pltpu.VMEM((pairs, 2, depth, out_cols), BF16),
+            pltpu.VMEM((2, pairs, 2, depth, out_cols), BF16),
             dma((2 * REACH + 1, 2)), dma((2,)), dma((2, 2)), dma((2,)),
             dma((2,)), dma((2,)), dma((2, n)), dma((2, n)), dma((2, pairs)), dma((7,)),
-            dma((pairs,)), dma((pairs,)), dma((pairs,)), dma((2, pairs)),
+            dma((pairs, 2)), dma((pairs, 2)), dma((pairs, 2)), dma((2, pairs, 2)),
         ],
         compiler_params=pltpu.CompilerParams(
             collective_id=0, has_side_effects=True, vmem_limit_bytes=63 * 2**20,

time: 71.8 us -> 68.6 us (0.955)
  Pallas kernels: 68.2 us -> 64.4 us
    pallas_call x1, Pallas kernels: 68.2 us -> 64.4 us  [fused(): pl.pallas_call(functools.partial(layer, n), out_shape=(jax.ShapeDtypeStru...]
where the time goes in v4:
time: 68.6 us; the launch traced here: 67.8 us
  Pallas kernels  64.4 us (94%)
  other arithmetic  1.92 us (3%)
  local copies, waits for them, and re-layouts  0.8 us (1%)
    pallas_call x1, Pallas kernels, fused(): pl.pallas_call(functools.partial(layer, n), out_shape=(jax.ShapeDtypeStru...  64.4 us
    mul x1, other arithmetic, fused(): return (output, total[:depth] * scale, total[depth:] * scale)  1.92 us

profile of v4, /device:TPU:0, one launch (start us, length us, event | category | flops | bytes accessed | tf_op | source)
XLA Modules:
  0.0 67.8 jit_solution(5940641848263561122)
XLA Ops:
  0.6 64.4 %shard_map.94 = (bf16[512,512]{1,0:T(8,128)(2,1)}, f32[256,512]{1,0:T(8,128)}) custom-call(bf16[4,128,512]{2,1,0:T(8,128)(2,1)} %bitcast.1, bf16[4,8,128,128]{3,2,1,0:T(8,128)(2,1)} %e_hbm.1, s32[4,8]{1,0:T(4,128)} %cols_ref.1, s32[4]{0:T(128)} %count_ref.1, bf16[128,512]{1,0:T(8,128)(2,1)} %ws_hbm.1, bf16[128,512]{1,0:T(8,128)(2,1)} %wn_hbm.1, ...), custom_call_target="tpu_custom_call" | custom-call | flops 2684354560 | bytes 2621440 | tf_op jit(solution)/shard_map/pallas_call | solution.py:365
  65.0 0.0 copy-start
  65.1 1.9 %slice_multiply_fusion = (f32[128,512]{1,0:T(8,128)}, f32[128,512]{1,0:T(8,128)}) fusion(f32[256,512]{1,0:T(8,128)} %get-tuple-element.6), kind=kLoop, calls=%fused_computation | loop fusion | flops 131072 | bytes 1048576 | tf_op jit(solution)/shard_map/mul | solution.py:402
  67.0 0.0 copy-done
  67.0 0.8 %copy.11 = bf16[512,512]{1,0:T(8,128)(2,1)} copy(bf16[512,512]{1,0:T(8,128)(2,1)S(1)} %copy-done) | data formatting | bytes 1048576
Async XLA Ops:
  65.0 1.9 %copy-start = (bf16[512,512]{1,0:T(8,128)(2,1)S(1)}, bf16[512,512]{1,0:T(8,128)(2,1)}, u32[]{:S(2)}) copy-start(bf16[512,512]{1,0:T(8,128)(2,1)} %get-tuple-element.12) | copy-start | bytes 1572868

commit v5 on v4

--- a/solution.py
+++ b/solution.py
@@ -11,6 +11,7 @@
 B = 128
 REACH = 2
 TILE = 128
+SHARES = 2
 
 
 def passed_along(array, axis, by):
@@ -310,14 +311,21 @@
             preferred_element_type=F32)
 
     dests = [dest_order(step, pair, pairs) for step in range(pairs)]
-    terms = [(step, dest, k) for step, dest in enumerate(dests) for k in (0, 1)]
+    terms = [(step, dest, k) for step, dest in enumerate(dests) for k in range(2 * SHARES)]
+    share = depth // SHARES
     for step, dest, k in terms:
-        xs[step, k] = gradient((full, agg)[k], 2 * dest + 1 - side).astype(BF16)
+        if k % SHARES == 0:
+            whole = gradient((full, agg)[k // SHARES], 2 * dest + 1 - side).astype(BF16)
+        at = k % SHARES * share
+        xs[step, k] = whole[at:at + share, :]
         send(None, lambda step=step, k=k: remote(
             xs.at[step, k], xr.at[step, k], x_send.at[step, k], x_recv.at[step, k],
             {"rows": partner}))
     for step, dest, k in terms:
-        part[step, k] = gradient((full, agg)[k], 2 * dest + side)
+        if k % SHARES == 0:
+            whole = gradient((full, agg)[k // SHARES], 2 * dest + side)
+        at = k % SHARES * share
+        part[step, k] = whole[at:at + share, :]
     for step, dest, k in terms:
         arrived(xr.at[step, k], x_recv.at[step, k])
         part[step, k] = part[step, k] + xr[step, k].astype(F32)
@@ -340,7 +348,7 @@
                 def _():
                     arrived(zr.at[way, pair, k], z_recv.at[way, pair, k])
                     part[step, k] = part[step, k] + zr[way, pair, k].astype(F32)
-            grad_ref[k * depth:(k + 1) * depth, :] = part[step, k]
+            grad_ref[k * share:(k + 1) * share, :] = part[step, k]
     store.wait()
 
     for cond, make in pending:
@@ -381,14 +389,15 @@
             pltpu.VMEM((blocks, B, B), F32),
             pltpu.VMEM((2, n * depth, out_cols), BF16),
             pltpu.VMEM((nodes, out_cols), BF16),
-            pltpu.VMEM((pairs, 2, depth, out_cols), F32),
-            pltpu.VMEM((pairs, 2, depth, out_cols), BF16),
-            pltpu.VMEM((pairs, 2, depth, out_cols), BF16),
-            pltpu.VMEM((pairs, 2, depth, out_cols), BF16),
-            pltpu.VMEM((2, pairs, 2, depth, out_cols), BF16),
+            pltpu.VMEM((pairs, 2 * SHARES, depth // SHARES, out_cols), F32),
+            pltpu.VMEM((pairs, 2 * SHARES, depth // SHARES, out_cols), BF16),
+            pltpu.VMEM((pairs, 2 * SHARES, depth // SHARES, out_cols), BF16),
+            pltpu.VMEM((pairs, 2 * SHARES, depth // SHARES, out_cols), BF16),
+            pltpu.VMEM((2, pairs, 2 * SHARES, depth // SHARES, out_cols), BF16),
             dma((2 * REACH + 1, 2)), dma((2,)), dma((2, 2)), dma((2,)),
             dma((2,)), dma((2,)), dma((2, n)), dma((2, n)), dma((2, pairs)), dma((7,)),
-            dma((pairs, 2)), dma((pairs, 2)), dma((pairs, 2)), dma((2, pairs, 2)),
+            dma((pairs, 2 * SHARES)), dma((pairs, 2 * SHARES)), dma((pairs, 2 * SHARES)),
+            dma((2, pairs, 2 * SHARES)),
         ],
         compiler_params=pltpu.CompilerParams(
             collective_id=0, has_side_effects=True, vmem_limit_bytes=63 * 2**20,

time: 68.6 us -> 68.7 us (level)
  no operation moved by 1% of the time
where the time goes in v5:
time: 68.7 us; the launch traced here: 68 us
  Pallas kernels  64.6 us (94%)
  other arithmetic  1.92 us (3%)
  local copies, waits for them, and re-layouts  0.8 us (1%)
    pallas_call x1, Pallas kernels, fused(): pl.pallas_call(functools.partial(layer, n), out_shape=(jax.ShapeDtypeStru...  64.6 us
    mul x1, other arithmetic, fused(): return (output, total[:depth] * scale, total[depth:] * scale)  1.92 us

profile of v5, /device:TPU:0, one launch (start us, length us, event | category | flops | bytes accessed | tf_op | source)
XLA Modules:
  0.0 68.0 jit_solution(14098132212768326129)
XLA Ops:
  0.6 64.6 %shard_map.94 = (bf16[512,512]{1,0:T(8,128)(2,1)}, f32[256,512]{1,0:T(8,128)}) custom-call(bf16[4,128,512]{2,1,0:T(8,128)(2,1)} %bitcast.1, bf16[4,8,128,128]{3,2,1,0:T(8,128)(2,1)} %e_hbm.1, s32[4,8]{1,0:T(4,128)} %cols_ref.1, s32[4]{0:T(128)} %count_ref.1, bf16[128,512]{1,0:T(8,128)(2,1)} %ws_hbm.1, bf16[128,512]{1,0:T(8,128)(2,1)} %wn_hbm.1, ...), custom_call_target="tpu_custom_call" | custom-call | flops 2684354560 | bytes 2621440 | tf_op jit(solution)/shard_map/pallas_call | solution.py:373
  65.3 0.0 copy-start
  65.3 1.9 %slice_multiply_fusion = (f32[128,512]{1,0:T(8,128)}, f32[128,512]{1,0:T(8,128)}) fusion(f32[256,512]{1,0:T(8,128)} %get-tuple-element.6), kind=kLoop, calls=%fused_computation | loop fusion | flops 131072 | bytes 1048576 | tf_op jit(solution)/shard_map/mul | solution.py:411
  67.2 0.0 copy-done
  67.2 0.8 %copy.11 = bf16[512,512]{1,0:T(8,128)(2,1)} copy(bf16[512,512]{1,0:T(8,128)(2,1)S(1)} %copy-done) | data formatting | bytes 1048576
Async XLA Ops:
  65.3 1.9 %copy-start = (bf16[512,512]{1,0:T(8,128)(2,1)S(1)}, bf16[512,512]{1,0:T(8,128)(2,1)}, u32[]{:S(2)}) copy-start(bf16[512,512]{1,0:T(8,128)(2,1)} %get-tuple-element.12) | copy-start | bytes 1572868
